TPU v7x, 32 devices: a whole 2x2x4 slice. The times are simulated.
32 devices in a mesh: seq: 4 (over z), dp: 8 (over y, x, core).
Axes of the slice: x: 2, y: 2, z: 4, core: 2. Of those that a mesh axis runs over, the one named last changes fastest.
Arguments:
- tokens: bfloat16 [8, 1024, 768], P('dp', 'seq'), may hold values from -6 to 6
- qkv_weight: bfloat16 [768, 2304], P('dp'), may hold values from -0.21875 to 0.21875
- proj_weight: bfloat16 [768, 768], P('dp'), may hold values from -0.875 to 0.875
- hidden_weight: bfloat16 [768, 3072], P('dp'), may hold values from -0.21875 to 0.21875
- output_weight: bfloat16 [3072, 768], P('dp'), may hold values from -0.109375 to 0.109375
- first_gain: bfloat16 [768], P('dp'), may hold values from 0.25 to 1.75
- first_bias: bfloat16 [768], P('dp'), may hold values from -2.5 to 2.5
- second_gain: bfloat16 [768], P('dp'), may hold values from 0.25 to 1.75
- second_bias: bfloat16 [768], P('dp'), may hold values from -2.5 to 2.5
- cotangent: bfloat16 [8, 1024, 768], P('dp', 'seq'), may hold values from -6 to 6
Outputs:
- block_out: bfloat16 [8, 1024, 768], P('dp', 'seq')
- tokens_gradient: bfloat16 [8, 1024, 768], P('dp', 'seq')
- qkv_gradient: float32 [768, 2304], P('dp')
- proj_gradient: float32 [768, 768], P('dp')
- hidden_gradient: float32 [768, 3072], P('dp')
- output_gradient: float32 [3072, 768], P('dp')
- first_gain_gradient: float32 [768], P('dp')
- first_bias_gradient: float32 [768], P('dp')
- second_gain_gradient: float32 [768], P('dp')
- second_bias_gradient: float32 [768], P('dp')
All inputs are finite; a program needn't handle non-finite values.
Results may differ from a plain program's by a relative error of at most 0.012.
Values may be sent and summed in bfloat16 or wider, within the bound.
A program may use at most 256 MiB of HBM per device.

v0:
```python
import jax
import jax.numpy as jnp
from jax import lax
from jax.sharding import PartitionSpec as P

HEAD_DIM = 64
LOW = jnp.bfloat16
F32 = jnp.float32


def layer_norm(values, gain, bias):
    average = jnp.mean(values, -1, keepdims=True)
    centred = values - average
    variance = jnp.mean(centred * centred, -1, keepdims=True)
    return centred * lax.rsqrt(variance + 1e-05) * gain + bias


def gelu_tanh(values):
    return jax.nn.gelu(values, approximate=True)


def matmul(left, right):
    return jnp.dot(left, right, preferred_element_type=F32)


def matmul_left_t(left, right):
    return lax.dot_general(left, right, (((0,), (0,)), ((), ())), preferred_element_type=F32)


def matmul_right_t(left, right):
    return lax.dot_general(left, right, (((1,), (1,)), ((), ())), preferred_element_type=F32)


def gather_seq(value):
    return lax.all_gather(value, "seq", axis=0, tiled=True)


def scatter_seq(value):
    return lax.psum_scatter(value.astype(LOW), "seq", scatter_dimension=0, tiled=True).astype(F32)


def attention_forward(queries, keys, values):
    length, local_width = queries.shape
    heads_here = local_width // HEAD_DIM
    block_rows = min(512, length)
    blocks = length // block_rows
    scale = HEAD_DIM ** (-0.5)
    outs, logs = ([], [])
    key_index = jnp.arange(length)
    for b in range(blocks):
        seen = (b + 1) * block_rows
        q = queries[b * block_rows : seen].reshape(block_rows, heads_here, HEAD_DIM)
        k = keys[:seen].reshape(seen, heads_here, HEAD_DIM)
        v = values[:seen].reshape(seen, heads_here, HEAD_DIM)
        raw = jnp.einsum("qhd,khd->hqk", q, k, preferred_element_type=F32)
        positions = b * block_rows + jnp.arange(block_rows)
        causal = key_index[None, :seen] <= positions[:, None]
        scores = jnp.where(causal[None], raw * scale, -1e30)
        largest = jnp.max(scores, -1, keepdims=True)
        expo = jnp.exp(scores - largest)
        total = jnp.sum(expo, -1, keepdims=True)
        probs = (expo / total).astype(LOW)
        context = jnp.einsum("hqk,khd->qhd", probs, v, preferred_element_type=F32)
        outs.append(context.astype(LOW).reshape(block_rows, local_width))
        logs.append(largest + jnp.log(total))
    return (jnp.concatenate(outs, axis=0), logs)


def attention_backward(queries, keys, values, grads, logs):
    length, local_width = queries.shape
    heads_here = local_width // HEAD_DIM
    block_rows = min(512, length)
    blocks = length // block_rows
    scale = HEAD_DIM ** (-0.5)
    key_index = jnp.arange(length)
    query_grads = []
    key_sum = jnp.zeros((length, heads_here, HEAD_DIM), F32)
    value_sum = jnp.zeros((length, heads_here, HEAD_DIM), F32)
    for b in range(blocks):
        seen = (b + 1) * block_rows
        q = queries[b * block_rows : seen].reshape(block_rows, heads_here, HEAD_DIM)
        g = grads[b * block_rows : seen].reshape(block_rows, heads_here, HEAD_DIM)
        k = keys[:seen].reshape(seen, heads_here, HEAD_DIM)
        v = values[:seen].reshape(seen, heads_here, HEAD_DIM)
        raw = jnp.einsum("qhd,khd->hqk", q, k, preferred_element_type=F32)
        positions = b * block_rows + jnp.arange(block_rows)
        causal = key_index[None, :seen] <= positions[:, None]
        scores = jnp.where(causal[None], raw * scale, -1e30)
        probs = jnp.exp(scores - logs[b])
        low_probs = probs.astype(LOW)
        value_term = jnp.einsum("hqk,qhd->khd", low_probs, g, preferred_element_type=F32)
        prob_grad = jnp.einsum("qhd,khd->hqk", g, v, preferred_element_type=F32)
        score_grad = (probs * (prob_grad - jnp.sum(probs * prob_grad, -1, keepdims=True))).astype(
            LOW
        )
        query_grad = jnp.einsum("hqk,khd->qhd", score_grad, k, preferred_element_type=F32) * scale
        key_term = jnp.einsum("hqk,qhd->khd", score_grad, q, preferred_element_type=F32) * scale
        pad = ((0, length - seen), (0, 0), (0, 0))
        key_sum = key_sum + jnp.pad(key_term, pad)
        value_sum = value_sum + jnp.pad(value_term, pad)
        query_grads.append(query_grad.astype(LOW).reshape(block_rows, local_width))
    return (
        jnp.concatenate(query_grads, axis=0),
        key_sum.astype(LOW).reshape(length, local_width),
        value_sum.astype(LOW).reshape(length, local_width),
    )


def on_device(
    tokens,
    qkv_weight,
    proj_weight,
    hidden_weight,
    output_weight,
    first_gain,
    first_bias,
    second_gain,
    second_bias,
    cotangent,
):
    parts = lax.axis_size("seq")
    groups = lax.axis_size("dp")
    part = lax.axis_index("seq")
    inputs_low = tokens[0]
    rows, width = inputs_low.shape
    model_rows = qkv_weight.shape[0]
    local_width = width // parts
    hidden_rows = output_weight.shape[0] // parts
    hidden_here = hidden_rows * groups
    qkv_here = lax.dynamic_index_in_dim(
        qkv_weight.reshape(model_rows, 3, parts, local_width), part, 2, keepdims=False
    ).reshape(model_rows, 3 * local_width)
    hidden_cols = lax.dynamic_index_in_dim(
        hidden_weight.reshape(model_rows, groups, parts, hidden_rows), part, 2, keepdims=False
    ).reshape(model_rows, hidden_here)
    output_here = lax.dynamic_slice_in_dim(output_weight, part * hidden_rows, hidden_rows, 0)
    norms = jnp.stack([first_gain, first_bias, second_gain, second_bias], axis=0)
    norms = lax.all_gather(norms, "dp", axis=1, tiled=True).astype(F32)
    gain_one, bias_one, gain_two, bias_two = (norms[0], norms[1], norms[2], norms[3])
    all_tokens = gather_seq(inputs_low)
    wide_qkv = lax.all_gather(qkv_here, "dp", axis=0, tiled=True)
    wide_proj = lax.all_gather(proj_weight, "dp", axis=0, tiled=True)
    wide_hidden = lax.all_gather(hidden_cols, "dp", axis=0, tiled=True)
    wide_output = lax.all_gather(output_here, "dp", axis=0, tiled=True)
    all_grads = gather_seq(cotangent[0])
    inputs = all_tokens.astype(F32)
    lowered_one = layer_norm(inputs, gain_one, bias_one).astype(LOW)
    projected = matmul(lowered_one, wide_qkv).astype(LOW)
    queries = projected[:, :local_width]
    keys = projected[:, local_width : 2 * local_width]
    values = projected[:, 2 * local_width :]
    context_here, logs = attention_forward(queries, keys, values)
    context = lax.all_gather(context_here, "seq", axis=1, tiled=True)
    middle = inputs + matmul(context, wide_proj)
    lowered_two = layer_norm(middle, gain_two, bias_two).astype(LOW)
    hidden_pre = matmul(lowered_two, wide_hidden)
    activated_float, gelu_pull = jax.vjp(gelu_tanh, hidden_pre)
    activated = activated_float.astype(LOW)
    act_grad = matmul_right_t(all_grads, wide_output)
    pre_grad = gelu_pull(act_grad)[0].astype(LOW)
    normed_two_grad = scatter_seq(matmul_right_t(pre_grad, wide_hidden))
    ffn_out = scatter_seq(matmul(activated, wide_output))
    middle_own = lax.dynamic_slice_in_dim(middle, part * rows, rows, 0)
    block_out = middle_own + ffn_out
    _, norm_pull_two = jax.vjp(layer_norm, middle_own, gain_two, bias_two)
    middle_part, gain_two_term, bias_two_term = norm_pull_two(normed_two_grad)
    middle_grad = cotangent[0].astype(F32) + middle_part
    attn_grad = gather_seq(middle_grad.astype(LOW))
    proj_here = lax.dynamic_slice_in_dim(wide_proj, part * local_width, local_width, 0)
    context_grad = matmul_right_t(attn_grad, proj_here).astype(LOW)
    query_grads, key_grads, value_grads = attention_backward(
        queries, keys, values, context_grad, logs
    )
    qkv_grad = jnp.concatenate([query_grads, key_grads, value_grads], axis=1)
    normed_one_grad = scatter_seq(matmul_right_t(qkv_grad, wide_qkv))
    _, norm_pull_one = jax.vjp(layer_norm, inputs_low.astype(F32), gain_one, bias_one)
    input_part, gain_one_term, bias_one_term = norm_pull_one(normed_one_grad)
    tokens_gradient = (middle_grad + input_part).astype(LOW)
    attn_cols = lax.dynamic_slice_in_dim(attn_grad, part * local_width, local_width, 1)
    output_term = matmul_left_t(activated, all_grads).astype(LOW)
    hidden_term = matmul_left_t(lowered_two, pre_grad).astype(LOW)
    proj_term = matmul_left_t(context, attn_cols).astype(LOW)
    qkv_term = matmul_left_t(lowered_one, qkv_grad).astype(LOW)
    first_terms = jnp.concatenate([output_term, hidden_term], axis=1)
    second_terms = jnp.concatenate([proj_term, qkv_term], axis=1)
    first_sum = lax.psum_scatter(first_terms, "dp", scatter_dimension=0, tiled=True)
    second_sum = lax.psum_scatter(second_terms, "dp", scatter_dimension=0, tiled=True)
    first_all = lax.all_gather(first_sum, "seq", axis=0)
    second_all = lax.all_gather(second_sum, "seq", axis=0)
    output_gradient = first_all[:, :, :width].reshape(parts * hidden_rows, width).astype(F32)
    hidden_gradient = (
        first_all[:, :, width:]
        .reshape(parts, model_rows, groups, hidden_rows)
        .transpose(1, 2, 0, 3)
        .reshape(model_rows, parts * hidden_here)
        .astype(F32)
    )
    proj_gradient = (
        second_all[:, :, :local_width].transpose(1, 0, 2).reshape(model_rows, width).astype(F32)
    )
    qkv_gradient = (
        second_all[:, :, local_width:]
        .reshape(parts, model_rows, 3, local_width)
        .transpose(1, 2, 0, 3)
        .reshape(model_rows, 3 * width)
        .astype(F32)
    )
    norm_terms = jnp.stack([gain_one_term, bias_one_term, gain_two_term, bias_two_term], axis=0)
    norm_sum = lax.psum(norm_terms, ("seq", "dp"))
    norm_own = lax.dynamic_slice_in_dim(
        norm_sum, lax.axis_index("dp") * first_gain.shape[0], first_gain.shape[0], 1
    )
    return (
        block_out.astype(LOW)[None],
        tokens_gradient[None],
        qkv_gradient,
        proj_gradient,
        hidden_gradient,
        output_gradient,
        norm_own[0],
        norm_own[1],
        norm_own[2],
        norm_own[3],
    )


def solution(mesh):
    placed = (
        P("dp", "seq", None),
        P("dp", None),
        P("dp", None),
        P("dp", None),
        P("dp", None),
        P("dp"),
        P("dp"),
        P("dp"),
        P("dp"),
        P("dp", "seq", None),
    )
    return jax.shard_map(
        on_device,
        mesh=mesh,
        in_specs=placed,
        out_specs=(
            P("dp", "seq", None),
            P("dp", "seq", None),
            P("dp", None),
            P("dp", None),
            P("dp", None),
            P("dp", None),
            P("dp"),
            P("dp"),
            P("dp"),
            P("dp"),
        ),
        check_vma=False,
    )
```

profile of v0, /device:TPU:0, one launch (start us, length us, event | category | flops | bytes accessed | tf_op | source)
XLA Modules:
  0.0 499.9 jit_solution(855848961846258834)
XLA Ops:
  10.8 10.3 %all-gather.4 = bf16[8,96,4]{1,2,0:T(4,128)(2,1)S(1)} all-gather(bf16[1,96,4]{1,2,0:T(4,128)(2,1)S(1)} %maximum_bitcast_fusion), channel_id=1, replica_groups=mesh['seq'=4,'dp'=8] {'dp'}, dimensions={0}, use_global_device_ids=true | all-gather | bytes 6912 | tf_op jit(solution)/shard_map/all_gather | solution.py:138
  24.7 11.9 %all_gather.41 = bf16[768,576]{1,0:T(8,128)(2,1)} all-gather(bf16[96,576]{1,0:T(8,128)(2,1)S(1)} %copy.126), channel_id=1, replica_groups=mesh['seq'=4,'dp'=8] {'dp'}, dimensions={0}, use_global_device_ids=true | all-gather | bytes 995328 | tf_op jit(solution)/shard_map/all_gather | solution.py:141
  36.7 13.9 %all-gather.24.cloned.1.call-done = bf16[1,1024,768]{1,2,0:T(8,128)(2,1)} async-done(((bf16[1,256,768]{1,2,0:T(8,128)(2,1)}), bf16[1,1024,768]{1,2,0:T(8,128)(2,1)}) %all-gather.24.cloned.1.call-update) | async-done | bytes 1572880 | tf_op jit(solution)/shard_map/all_gather | solution.py:35
  69.1 5.8 %all-gather.16.cloned.1.call-done = bf16[768,768]{1,0:T(8,128)(2,1)} async-done(((bf16[96,768]{1,0:T(8,128)(2,1)}), bf16[768,768]{1,0:T(8,128)(2,1)}) %all-gather.16.cloned.1.call-update) | async-done | bytes 1179664 | tf_op jit(solution)/shard_map/all_gather | solution.py:142
  74.8 39.3 %all-gather.14.cloned.1.call-done = bf16[1024,768]{0,1:T(8,128)(2,1)} async-done(((bf16[1024,192]{0,1:T(8,128)(2,1)}), bf16[1024,768]{0,1:T(8,128)(2,1)}) %all-gather.14.cloned.1.call-update) | async-done | bytes 1572880 | tf_op jit(solution)/shard_map/all_gather | solution.py:153
  114.1 3.7 fusion.90
  120.2 19.2 %all-gather.18.cloned.1.call-done = bf16[768,768]{1,0:T(8,128)(2,1)} async-done(((bf16[96,768]{1,0:T(8,128)(2,1)}), bf16[768,768]{1,0:T(8,128)(2,1)}) %all-gather.18.cloned.1.call-update) | async-done | bytes 1179664 | tf_op jit(solution)/shard_map/all_gather | solution.py:143
  139.4 4.8 fusion.91
  144.2 21.0 %all-gather.20.cloned.1.call-done = bf16[768,768]{1,0:T(8,128)(2,1)} async-done(((bf16[96,768]{1,0:T(8,128)(2,1)}), bf16[768,768]{1,0:T(8,128)(2,1)}) %all-gather.20.cloned.1.call-update) | async-done | bytes 1179664 | tf_op jit(solution)/shard_map/all_gather | solution.py:144
  165.2 38.5 %all-gather.26.cloned.1.call-done = bf16[1,1024,768]{2,1,0:T(8,128)(2,1)} async-done(((bf16[1,256,768]{2,1,0:T(8,128)(2,1)}), bf16[1,1024,768]{2,1,0:T(8,128)(2,1)}) %all-gather.26.cloned.1.call-update) | async-done | bytes 1572880 | tf_op jit(solution)/shard_map/all_gather | solution.py:35
  203.8 5.6 %fusion.16 = bf16[1024,768]{1,0:T(8,128)(2,1)S(1)} fusion(f32[1024,768]{1,0:T(8,128)} %fusion.91, bf16[768,768]{1,0:T(8,128)(2,1)} %all-gather.20.cloned.1.call-done, bf16[1,1024,768]{2,1,0:T(8,128)(2,1)} %all-gather.26.cloned.1.call-done), kind=kOutput, calls=%fused_computation.26 | convolution fusion | flops 1223688192 | bytes 7471104 | tf_op jit(solution)/shard_map/dot_general | solution.py:31
  210.5 2.6 convolution_convert_fusion.1
  213.4 3.5 convolution_convert_fusion.3
  220.2 4.3 copy.156
  227.2 20.3 %reduce-scatter.12.cloned.1.call-done = bf16[256,768]{0,1:T(8,128)(2,1)} async-done(((bf16[1024,768]{0,1:T(8,128)(2,1)}), bf16[256,768]{0,1:T(8,128)(2,1)}) %reduce-scatter.12.cloned.1.call-update) | async-done | bytes 393232 | tf_op jit(solution)/shard_map/reduce_scatter | solution.py:39
  247.5 2.0 multiply_reduce_fusion.3
  249.5 2.1 fusion.67
  252.2 2.7 fusion.70
  257.0 35.3 %reduce-scatter.18.cloned.1.call-done = bf16[96,1536]{1,0:T(8,128)(2,1)} async-done(((bf16[768,1536]{1,0:T(8,128)(2,1)}), bf16[96,1536]{1,0:T(8,128)(2,1)}) %reduce-scatter.18.cloned.1.call-update) | async-done | bytes 294928 | tf_op jit(solution)/shard_map/reduce_scatter | solution.py:186
  292.4 39.9 %all-gather.22.cloned.1.call-done = bf16[1024,768]{0,1:T(8,128)(2,1)} async-done(((bf16[256,768]{0,1:T(8,128)(2,1)}), bf16[1024,768]{0,1:T(8,128)(2,1)}) %all-gather.22.cloned.1.call-update) | async-done | bytes 1572880 | tf_op jit(solution)/shard_map/all_gather | solution.py:35
  332.3 2.0 convolution_convert_fusion.6
  351.5 2.5 convolution_convert_fusion
  354.3 5.0 %convolution_convert_fusion.2 = bf16[1024,768]{0,1:T(8,128)(2,1)} fusion(bf16[768,768]{1,0:T(8,128)(2,1)} %all-gather.20.cloned.1.call-done, f32[1024,768]{1,0:T(8,128)} %fusion.91), kind=kOutput, calls=%fused_computation.50 | convolution fusion | flops 1215823872 | bytes 5898240 | tf_op jit(solution)/shard_map/dot_general | solution.py:23
  362.5 2.4 fusion.84
  366.9 2.2 copy.143
  369.0 3.6 reshape.282
  373.8 28.3 %reduce-scatter.16.cloned.1.call-done = bf16[96,768]{1,0:T(8,128)(2,1)} async-done(((bf16[768,768]{1,0:T(8,128)(2,1)}), bf16[96,768]{1,0:T(8,128)(2,1)}) %reduce-scatter.16.cloned.1.call-update) | async-done | bytes 147472 | tf_op jit(solution)/shard_map/reduce_scatter | solution.py:187
  402.0 22.2 %all-gather.2 = bf16[384,768]{1,0:T(8,128)(2,1)S(1)} all-gather(bf16[96,768]{1,0:T(8,128)(2,1)} %reduce-scatter.16.cloned.1.call-done), channel_id=4, replica_groups=mesh['seq'=4,'dp'=8] {'seq'}, dimensions={0}, use_global_device_ids=true | all-gather | bytes 737280 | tf_op jit(solution)/shard_map/all_gather | solution.py:189
  427.8 2.9 reshape.280
  430.7 13.6 %reduce-scatter.14.cloned.1.call-done = bf16[256,768]{0,1:T(8,128)(2,1)} async-done(((bf16[1024,768]{0,1:T(8,128)(2,1)}), bf16[256,768]{0,1:T(8,128)(2,1)}) %reduce-scatter.14.cloned.1.call-update) | async-done | bytes 393232 | tf_op jit(solution)/shard_map/reduce_scatter | solution.py:39
  447.3 41.4 %psum.7 = f32[4,768]{1,0:T(4,128)S(1)} all-reduce(f32[4,768]{1,0:T(4,128)S(1)} %pad_maximum_fusion.6), channel_id=1, replica_groups=mesh['seq'=4,'dp'=8] {'seq','dp'}, use_global_device_ids=true, to_apply=%region_27.28 | all-reduce | flops 3072 | bytes 24576 | tf_op jit(solution)/shard_map/psum | solution.py:209
  489.3 2.0 fusion.73
  (228 shorter events, 70.0 us)
Async XLA Ops:
  7.2 60.5 %copy-start = (bf16[384,768]{1,0:T(8,128)(2,1)S(1)}, bf16[384,768]{1,0:T(8,128)(2,1)}, u32[]{:S(2)}) copy-start(bf16[384,768]{1,0:T(8,128)(2,1)} %param.14) | copy-start | bytes 1769476
  7.2 43.4 %all-gather.24.cloned.1.call-start = ((), (), s32[]{:S(2)}) async-start(), calls=%async_computation.13 | async-start | bytes 1966080 | tf_op jit(solution)/shard_map/all_gather | solution.py:35
  9.2 65.6 %all-gather.16.cloned.1.call-start = ((), (), s32[]{:S(2)}) async-start(), calls=%async_computation.6 | async-start | bytes 1327104 | tf_op jit(solution)/shard_map/all_gather | solution.py:142
  10.0 104.1 %all-gather.14.cloned.1.call-start = ((), (), s32[]{:S(2)}) async-start(), calls=%async_computation.5 | async-start | bytes 1966080 | tf_op jit(solution)/shard_map/all_gather | solution.py:153
  21.8 32.5 %copy-start.47 = (f32[768]{0:T(1024)}, f32[768]{0:T(1024)S(1)}, u32[]{:S(2)}) copy-start(f32[768]{0:T(1024)S(1)} %get-tuple-element.82) | copy-start | bytes 9220
  64.2 75.2 %all-gather.18.cloned.1.call-start = ((), (), s32[]{:S(2)}) async-start(), calls=%async_computation.7 | async-start | bytes 1327104 | tf_op jit(solution)/shard_map/all_gather | solution.py:143
  67.6 97.6 %all-gather.20.cloned.1.call-start = ((), (), s32[]{:S(2)}) async-start(), calls=%async_computation.8 | async-start | bytes 1327104 | tf_op jit(solution)/shard_map/all_gather | solution.py:144
  68.4 135.3 %all-gather.26.cloned.1.call-start = ((), (), s32[]{:S(2)}) async-start(), calls=%async_computation.14 | async-start | bytes 1966080 | tf_op jit(solution)/shard_map/all_gather | solution.py:35
  69.0 178.5 %reduce-scatter.12.cloned.1.call-start = ((), (), s32[]{:S(2)}) async-start(), calls=%async_computation.10 | async-start | bytes 1966080 | tf_op jit(solution)/shard_map/reduce_scatter | solution.py:39
  117.9 131.6 %copy-start.5 = (f32[1024,768]{0,1:T(8,128)}, f32[1024,768]{0,1:T(8,128)S(1)}, u32[]{:S(2)}) copy-start(f32[1024,768]{0,1:T(8,128)S(1)} %get-tuple-element.109) | copy-start | bytes 9437188
  203.8 6.8 %copy-start.53 = (bf16[768,768]{1,0:T(8,128)(2,1)S(1)}, bf16[768,768]{1,0:T(8,128)(2,1)}, u32[]{:S(2)}) copy-start(bf16[768,768]{1,0:T(8,128)(2,1)} %all-gather.18.cloned.1.call-done) | copy-start | bytes 3538948
  213.2 79.1 %reduce-scatter.18.cloned.1.call-start = ((), (), s32[]{:S(2)}) async-start(), calls=%async_computation.17 | async-start | bytes 2654208 | tf_op jit(solution)/shard_map/reduce_scatter | solution.py:186
  224.5 107.8 %all-gather.22.cloned.1.call-start = ((), (), s32[]{:S(2)}) async-start(), calls=%async_computation.11 | async-start | bytes 1966080 | tf_op jit(solution)/shard_map/all_gather | solution.py:35
  251.6 82.8 %copy-start.4 = (f32[3,512,512]{1,2,0:T(8,128)S(1)}, f32[3,512,512]{1,2,0:T(8,128)}, u32[]{:S(2)}) copy-start(f32[3,512,512]{1,2,0:T(8,128)} %copy-done.3) | copy-start | bytes 9437188
  254.9 107.6 %all-gather.28.cloned.1.call-start = ((), (), s32[]{:S(2)}) async-start(), calls=%async_computation.15 | async-start | bytes 1474560 | tf_op jit(solution)/shard_map/all_gather | solution.py:188
  292.3 109.7 %reduce-scatter.16.cloned.1.call-start = ((), (), s32[]{:S(2)}) async-start(), calls=%async_computation.16 | async-start | bytes 1327104 | tf_op jit(solution)/shard_map/reduce_scatter | solution.py:187
  337.4 10.9 %copy-start.26 = (bf16[3,64,512]{2,1,0:T(8,128)(2,1)}, bf16[3,64,512]{2,1,0:T(8,128)(2,1)S(1)}, u32[]{:S(2)}) copy-start(bf16[3,64,512]{2,1,0:T(8,128)(2,1)S(1)} %fusion.52) | copy-start | bytes 589828
  351.4 92.9 %reduce-scatter.14.cloned.1.call-start = ((), (), s32[]{:S(2)}) async-start(), calls=%async_computation.12 | async-start | bytes 1966080 | tf_op jit(solution)/shard_map/reduce_scatter | solution.py:39
  354.1 5.4 %copy-start.6 = (bf16[1,256,768]{1,2,0:T(8,128)(2,1)S(1)}, bf16[1,256,768]{1,2,0:T(8,128)(2,1)}, u32[]{:S(2)}) copy-start(bf16[1,256,768]{1,2,0:T(8,128)(2,1)} %copy.123) | copy-start | bytes 1179652
  354.1 6.0 %copy-start.34 = (f32[768]{0:T(1024)S(1)}, f32[768]{0:T(1024)}, u32[]{:S(2)}) copy-start(f32[768]{0:T(1024)} %get-tuple-element.79) | copy-start | bytes 9220
  354.1 6.6 %copy-start.35 = (f32[768]{0:T(1024)S(1)}, f32[768]{0:T(1024)}, u32[]{:S(2)}) copy-start(f32[768]{0:T(1024)} %get-tuple-element.70) | copy-start | bytes 9220
  354.1 135.2 %reduce-scatter.10.cloned.1.call-start = ((), (), s32[]{:S(2)}) async-start(), calls=%async_computation.9 | async-start | bytes 1966080 | tf_op jit(solution)/shard_map/reduce_scatter | solution.py:39
  426.1 18.2 %copy-start.38 = (f32[256]{0:T(256)S(1)}, f32[256]{0:T(256)}, u32[]{:S(2)}) copy-start(f32[256]{0:T(256)} %broadcast_multiply_fusion.2) | copy-start | bytes 3076
  426.1 21.1 %copy-start.43 = (f32[1,768]{1,0:T(1,128)S(1)}, f32[1,768]{1,0:T(1,128)}, u32[]{:S(2)}) copy-start(f32[1,768]{1,0:T(1,128)} %reshape.279) | copy-start | bytes 9220
  426.1 21.1 %copy-start.44 = (f32[1,768]{1,0:T(1,128)S(1)}, f32[1,768]{1,0:T(1,128)}, u32[]{:S(2)}) copy-start(f32[1,768]{1,0:T(1,128)} %reshape.278) | copy-start | bytes 9220
  426.2 63.1 %copy-start.9 = (bf16[256,768]{0,1:T(8,128)(2,1)S(1)}, bf16[256,768]{0,1:T(8,128)(2,1)}, u32[]{:S(2)}) copy-start(bf16[256,768]{0,1:T(8,128)(2,1)} %reduce-scatter.12.cloned.1.call-done) | copy-start | bytes 1179652
  426.2 63.1 %copy-start.10 = (bf16[1,256,768]{1,2,0:T(8,128)(2,1)S(1)}, bf16[1,256,768]{1,2,0:T(8,128)(2,1)}, u32[]{:S(2)}) copy-start(bf16[1,256,768]{1,2,0:T(8,128)(2,1)} %copy.130) | copy-start | bytes 1179652
  426.2 63.1 %copy-start.32 = (f32[256]{0:T(256)S(1)}, f32[256]{0:T(256)}, u32[]{:S(2)}) copy-start(f32[256]{0:T(256)} %broadcast_multiply_fusion.3) | copy-start | bytes 3076
  426.2 63.1 %copy-start.40 = (f32[256]{0:T(256)S(1)}, f32[256]{0:T(256)}, u32[]{:S(2)}) copy-start(f32[256]{0:T(256)} %copy-done.39) | copy-start | bytes 3076
  426.2 63.1 %copy-start.42 = (f32[256]{0:T(256)S(1)}, f32[256]{0:T(256)}, u32[]{:S(2)}) copy-start(f32[256]{0:T(256)} %copy-done.41) | copy-start | bytes 3076
  426.2 63.1 %copy-start.46 = (f32[256]{0:T(256)S(1)}, f32[256]{0:T(256)}, u32[]{:S(2)}) copy-start(f32[256]{0:T(256)} %copy-done.45) | copy-start | bytes 3076
  444.3 48.9 %copy-start.1 = (bf16[384,768]{1,0:T(8,128)(2,1)S(1)}, bf16[384,768]{1,0:T(8,128)(2,1)}, u32[]{:S(2)}) copy-start(bf16[384,768]{1,0:T(8,128)(2,1)} %param.14) | copy-start | bytes 1769476
  (39 other events, 92.1 us)
Sparse Core Ops, SparseCore 0:
  10.2 40.3 all-gather.23
  52.5 22.3 all-gather.15
  77.0 37.0 all-gather.13
  116.4 22.9 all-gather.17
  141.1 24.0 all-gather.19
  166.6 37.0 all-gather.25
  213.3 34.1 reduce-scatter.11
  250.8 41.4 reduce-scatter.17
  294.5 37.6 all-gather.21
  333.8 28.7 all-gather.27
  366.1 35.8 reduce-scatter.15
  404.2 40.0 reduce-scatter.13
  446.6 35.2 reduce-scatter.9
where the time goes:
time: 508 us; the launch traced here: 500 us
  waiting for transfers between devices  278 us (55%)
  blocking collectives  85.8 us (17%)
  matrix products  48.4 us (10%)
  local copies, waits for them, and re-layouts  38.9 us (8%)
  other arithmetic  32.6 us (6%)
  between operations  15.1 us (3%)
    all_gather x3, waiting for transfers between devices, gather_seq(): return lax.all_gather(value, 'seq', axis=0, tiled=True)  92.4 us
    psum x1, blocking collectives, on_device(): norm_sum = lax.psum(norm_terms, ('seq', 'dp'))  41.4 us
    all_gather x1, waiting for transfers between devices, on_device(): context = lax.all_gather(context_here, 'seq', axis=1, tiled=True)  39.3 us
    reduce_scatter x1, waiting for transfers between devices, on_device(): lax.psum_scatter(first_terms, 'dp', scatter_dimension=0, tiled=True)  35.3 us
    reduce_scatter x3, waiting for transfers between devices, scatter_seq(): lax.psum_scatter(value.astype(LOW), 'seq', scatter_dimension=0, tiled=True)  33.9 us
    reduce_scatter x1, waiting for transfers between devices, on_device(): lax.psum_scatter(second_terms, 'dp', scatter_dimension=0, tiled=True)  28.3 us
    all_gather x1, blocking collectives, on_device(): second_all = lax.all_gather(second_sum, 'seq', axis=0)  22.2 us
    all_gather x1, waiting for transfers between devices, on_device(): wide_output = lax.all_gather(output_here, 'dp', axis=0, tiled=True)  21 us
  transfers between devices with their start and end apart: 13, of which 12 were waited for; matrix products, arithmetic and copies ran while one was open for 20% of the time, Pallas kernels for 0%

commit v1 on v0

--- a/solution.py
+++ b/solution.py
@@ -2,6 +2,7 @@
 import jax.numpy as jnp
 from jax import lax
 from jax.sharding import PartitionSpec as P
+from jax.lax import all_gather
 
 HEAD_DIM = 64
 LOW = jnp.bfloat16
@@ -138,8 +139,13 @@
     norms = lax.all_gather(norms, "dp", axis=1, tiled=True).astype(F32)
     gain_one, bias_one, gain_two, bias_two = (norms[0], norms[1], norms[2], norms[3])
     all_tokens = gather_seq(inputs_low)
-    wide_qkv = lax.all_gather(qkv_here, "dp", axis=0, tiled=True)
-    wide_proj = lax.all_gather(proj_weight, "dp", axis=0, tiled=True)
+
+    def draw_the_values(mine, sample):
+        prior = jnp.concatenate([mine, sample], axis=1)
+        piece_out = all_gather(prior, "dp", axis=0, tiled=True)
+        return jnp.split(piece_out, [mine.shape[1]], axis=1)
+
+    wide_qkv, wide_proj = draw_the_values(qkv_here, proj_weight)
     wide_hidden = lax.all_gather(hidden_cols, "dp", axis=0, tiled=True)
     wide_output = lax.all_gather(output_here, "dp", axis=0, tiled=True)
     all_grads = gather_seq(cotangent[0])

time: 508 us -> 524 us (1.031)
  waiting for transfers between devices: 278 us -> 298 us
  blocking collectives: 85.8 us -> 73.9 us
    all_gather x1, waiting for transfers between devices: 5.78 us -> 25.2 us  [draw_the_values(): piece_out = all_gather(prior, 'dp', axis=0, tiled=True)]
    all_gather x1 -> x0, blocking collectives: 11.9 us -> none  [on_device(): wide_qkv = lax.all_gather(qkv_here, 'dp', axis=0, tiled=True)]
    all_gather x3, waiting for transfers between devices: 92.4 us -> 104 us  [gather_seq(): return lax.all_gather(value, 'seq', axis=0, tiled=True)]
    all_gather x1, waiting for transfers between devices: 39.3 us -> 32.5 us  [on_device(): context = lax.all_gather(context_here, 'seq', axis=1, tiled=True)]
    unnamed x123 -> x133, local copies, waits for them, and re-layouts: 16.8 us -> 18.3 us
  transfers between devices with their start and end apart: 13 -> 13, of which waited for: 12 -> 12; matrix products, arithmetic and copies ran while one was open for 20% -> 19% of each run, Pallas kernels for 0% -> 0%
where the time goes in v1:
time: 524 us; the launch traced here: 516 us
  waiting for transfers between devices  298 us (57%)
  blocking collectives  73.9 us (14%)
  matrix products  50.8 us (10%)
  local copies, waits for them, and re-layouts  43.5 us (8%)
  other arithmetic  32.8 us (6%)
  between operations  15.2 us (3%)
    all_gather x3, waiting for transfers between devices, gather_seq(): return lax.all_gather(value, 'seq', axis=0, tiled=True)  104 us
    psum x1, blocking collectives, on_device(): norm_sum = lax.psum(norm_terms, ('seq', 'dp'))  41.4 us
    reduce_scatter x3, waiting for transfers between devices, scatter_seq(): lax.psum_scatter(value.astype(LOW), 'seq', scatter_dimension=0, tiled=True)  33.9 us
    reduce_scatter x1, waiting for transfers between devices, on_device(): lax.psum_scatter(first_terms, 'dp', scatter_dimension=0, tiled=True)  32.8 us
    all_gather x1, waiting for transfers between devices, on_device(): context = lax.all_gather(context_here, 'seq', axis=1, tiled=True)  32.5 us
    reduce_scatter x1, waiting for transfers between devices, on_device(): lax.psum_scatter(second_terms, 'dp', scatter_dimension=0, tiled=True)  28.3 us
    all_gather x1, waiting for transfers between devices, draw_the_values(): piece_out = all_gather(prior, 'dp', axis=0, tiled=True)  25.2 us
    all_gather x1, blocking collectives, on_device(): second_all = lax.all_gather(second_sum, 'seq', axis=0)  22.2 us
  transfers between devices with their start and end apart: 13, of which 12 were waited for; matrix products, arithmetic and copies ran while one was open for 19% of the time, Pallas kernels for 0%

profile of v1, /device:TPU:0, one launch (start us, length us, event | category | flops | bytes accessed | tf_op | source)
XLA Modules:
  0.0 515.7 jit_solution(452102896286852603)
XLA Ops:
  7.3 2.0 copy.127
  12.7 10.3 %all-gather.4 = bf16[8,96,4]{1,2,0:T(4,128)(2,1)S(1)} all-gather(bf16[1,96,4]{1,2,0:T(4,128)(2,1)S(1)} %maximum_bitcast_fusion), channel_id=1, replica_groups=mesh['seq'=4,'dp'=8] {'dp'}, dimensions={0}, use_global_device_ids=true | all-gather | bytes 6912 | tf_op jit(solution)/shard_map/all_gather | solution.py:139
  25.0 25.6 %all-gather.24.cloned.1.call-done = bf16[1,1024,768]{1,2,0:T(8,128)(2,1)} async-done(((bf16[1,256,768]{1,2,0:T(8,128)(2,1)}), bf16[1,1024,768]{1,2,0:T(8,128)(2,1)}) %all-gather.24.cloned.1.call-update) | async-done | bytes 1572880 | tf_op jit(solution)/shard_map/all_gather | solution.py:36
  54.4 25.2 %all-gather.14.cloned.1.call-done = bf16[768,1344]{1,0:T(8,128)(2,1)} async-done(((bf16[96,1344]{1,0:T(8,128)(2,1)}), bf16[768,1344]{1,0:T(8,128)(2,1)}) %all-gather.14.cloned.1.call-update) | async-done | bytes 2064400 | tf_op jit(solution)/shard_map/all_gather | solution.py:145
  79.6 2.5 convolution_convert_fusion.4
  96.8 32.5 %all-gather.16.cloned.1.call-done = bf16[1024,768]{0,1:T(8,128)(2,1)} async-done(((bf16[1024,192]{0,1:T(8,128)(2,1)}), bf16[1024,768]{0,1:T(8,128)(2,1)}) %all-gather.16.cloned.1.call-update) | async-done | bytes 1572880 | tf_op jit(solution)/shard_map/all_gather | solution.py:159
  129.3 4.1 fusion.93
  135.8 18.8 %all-gather.18.cloned.1.call-done = bf16[768,768]{1,0:T(8,128)(2,1)} async-done(((bf16[96,768]{1,0:T(8,128)(2,1)}), bf16[768,768]{1,0:T(8,128)(2,1)}) %all-gather.18.cloned.1.call-update) | async-done | bytes 1179664 | tf_op jit(solution)/shard_map/all_gather | solution.py:149
  154.6 4.8 fusion.94
  159.4 21.6 %all-gather.20.cloned.1.call-done = bf16[768,768]{1,0:T(8,128)(2,1)} async-done(((bf16[96,768]{1,0:T(8,128)(2,1)}), bf16[768,768]{1,0:T(8,128)(2,1)}) %all-gather.20.cloned.1.call-update) | async-done | bytes 1179664 | tf_op jit(solution)/shard_map/all_gather | solution.py:150
  181.0 38.5 %all-gather.26.cloned.1.call-done = bf16[1,1024,768]{2,1,0:T(8,128)(2,1)} async-done(((bf16[1,256,768]{2,1,0:T(8,128)(2,1)}), bf16[1,1024,768]{2,1,0:T(8,128)(2,1)}) %all-gather.26.cloned.1.call-update) | async-done | bytes 1572880 | tf_op jit(solution)/shard_map/all_gather | solution.py:36
  219.5 5.6 %fusion.16 = bf16[1024,768]{1,0:T(8,128)(2,1)S(1)} fusion(f32[1024,768]{1,0:T(8,128)} %fusion.94, bf16[768,768]{1,0:T(8,128)(2,1)} %all-gather.20.cloned.1.call-done, bf16[1,1024,768]{2,1,0:T(8,128)(2,1)} %all-gather.26.cloned.1.call-done), kind=kOutput, calls=%fused_computation.26 | convolution fusion | flops 1223688192 | bytes 7471104 | tf_op jit(solution)/shard_map/dot_general | solution.py:32
  226.3 2.6 convolution_convert_fusion.1
  229.1 3.5 convolution_convert_fusion.3
  235.9 4.3 copy.160
  242.9 20.3 %reduce-scatter.12.cloned.1.call-done = bf16[256,768]{0,1:T(8,128)(2,1)} async-done(((bf16[1024,768]{0,1:T(8,128)(2,1)}), bf16[256,768]{0,1:T(8,128)(2,1)}) %reduce-scatter.12.cloned.1.call-update) | async-done | bytes 393232 | tf_op jit(solution)/shard_map/reduce_scatter | solution.py:40
  265.2 2.1 fusion.69
  267.9 2.2 fusion.72
  270.1 3.1 split.9
  275.2 32.8 %reduce-scatter.18.cloned.1.call-done = bf16[96,1536]{1,0:T(8,128)(2,1)} async-done(((bf16[768,1536]{1,0:T(8,128)(2,1)}), bf16[96,1536]{1,0:T(8,128)(2,1)}) %reduce-scatter.18.cloned.1.call-update) | async-done | bytes 294928 | tf_op jit(solution)/shard_map/reduce_scatter | solution.py:192
  308.3 39.7 %all-gather.22.cloned.1.call-done = bf16[1024,768]{0,1:T(8,128)(2,1)} async-done(((bf16[256,768]{0,1:T(8,128)(2,1)}), bf16[1024,768]{0,1:T(8,128)(2,1)}) %all-gather.22.cloned.1.call-update) | async-done | bytes 1572880 | tf_op jit(solution)/shard_map/all_gather | solution.py:36
  348.0 2.0 convolution_convert_fusion.6
  367.2 3.8 convolution_convert_fusion
  371.4 4.6 convolution_convert_fusion.2
  378.2 2.4 fusion.87
  382.6 2.2 copy.147
  384.7 3.6 reshape.282
  389.5 28.3 %reduce-scatter.16.cloned.1.call-done = bf16[96,768]{1,0:T(8,128)(2,1)} async-done(((bf16[768,768]{1,0:T(8,128)(2,1)}), bf16[96,768]{1,0:T(8,128)(2,1)}) %reduce-scatter.16.cloned.1.call-update) | async-done | bytes 147472 | tf_op jit(solution)/shard_map/reduce_scatter | solution.py:193
  417.8 22.2 %all-gather.2 = bf16[384,768]{1,0:T(8,128)(2,1)S(1)} all-gather(bf16[96,768]{1,0:T(8,128)(2,1)} %reduce-scatter.16.cloned.1.call-done), channel_id=4, replica_groups=mesh['seq'=4,'dp'=8] {'seq'}, dimensions={0}, use_global_device_ids=true | all-gather | bytes 737280 | tf_op jit(solution)/shard_map/all_gather | solution.py:195
  443.5 2.9 reshape.280
  446.4 13.6 %reduce-scatter.14.cloned.1.call-done = bf16[256,768]{0,1:T(8,128)(2,1)} async-done(((bf16[1024,768]{0,1:T(8,128)(2,1)}), bf16[256,768]{0,1:T(8,128)(2,1)}) %reduce-scatter.14.cloned.1.call-update) | async-done | bytes 393232 | tf_op jit(solution)/shard_map/reduce_scatter | solution.py:40
  463.0 41.4 %psum.7 = f32[4,768]{1,0:T(4,128)S(1)} all-reduce(f32[4,768]{1,0:T(4,128)S(1)} %pad_maximum_fusion.7), channel_id=1, replica_groups=mesh['seq'=4,'dp'=8] {'seq','dp'}, use_global_device_ids=true, to_apply=%region_27.28 | all-reduce | flops 3072 | bytes 24576 | tf_op jit(solution)/shard_map/psum | solution.py:215
  (239 shorter events, 71.5 us)
Async XLA Ops:
  7.2 88.3 %copy-start = (bf16[384,768]{1,0:T(8,128)(2,1)S(1)}, bf16[384,768]{1,0:T(8,128)(2,1)}, u32[]{:S(2)}) copy-start(bf16[384,768]{1,0:T(8,128)(2,1)} %param.14) | copy-start | bytes 1769476
  7.2 43.4 %all-gather.24.cloned.1.call-start = ((), (), s32[]{:S(2)}) async-start(), calls=%async_computation.13 | async-start | bytes 1966080 | tf_op jit(solution)/shard_map/all_gather | solution.py:36
  9.3 70.2 %all-gather.14.cloned.1.call-start = ((), (), s32[]{:S(2)}) async-start(), calls=%async_computation.5 | async-start | bytes 2433024 | tf_op jit(solution)/shard_map/all_gather | solution.py:145
  12.6 116.8 %all-gather.16.cloned.1.call-start = ((), (), s32[]{:S(2)}) async-start(), calls=%async_computation.6 | async-start | bytes 1966080 | tf_op jit(solution)/shard_map/all_gather | solution.py:159
  23.7 55.8 %copy-start.47 = (f32[768]{0:T(1024)}, f32[768]{0:T(1024)S(1)}, u32[]{:S(2)}) copy-start(f32[768]{0:T(1024)S(1)} %get-tuple-element.82) | copy-start | bytes 9220
  50.7 28.9 %copy-start.7 = (bf16[1,1024,768]{1,2,0:T(8,128)(2,1)S(1)}, bf16[1,1024,768]{1,2,0:T(8,128)(2,1)}, u32[]{:S(2)}) copy-start(bf16[1,1024,768]{1,2,0:T(8,128)(2,1)} %all-gather.24.cloned.1.call-done) | copy-start | bytes 4718596
  52.5 29.6 %copy-start.36 = (f32[1024]{0:T(1024)}, f32[1024]{0:T(1024)S(1)}, u32[]{:S(2)}) copy-start(f32[1024]{0:T(1024)S(1)} %broadcast_multiply_fusion.1) | copy-start | bytes 12292
  54.3 25.2 %copy-start.49 = (f32[1024]{0:T(1024)}, f32[1024]{0:T(1024)S(1)}, u32[]{:S(2)}) copy-start(f32[1024]{0:T(1024)S(1)} %add_rsqrt_fusion.1) | copy-start | bytes 12292
  92.0 62.5 %all-gather.18.cloned.1.call-start = ((), (), s32[]{:S(2)}) async-start(), calls=%async_computation.7 | async-start | bytes 1327104 | tf_op jit(solution)/shard_map/all_gather | solution.py:149
  95.5 85.5 %all-gather.20.cloned.1.call-start = ((), (), s32[]{:S(2)}) async-start(), calls=%async_computation.8 | async-start | bytes 1327104 | tf_op jit(solution)/shard_map/all_gather | solution.py:150
  96.2 123.3 %all-gather.26.cloned.1.call-start = ((), (), s32[]{:S(2)}) async-start(), calls=%async_computation.14 | async-start | bytes 1966080 | tf_op jit(solution)/shard_map/all_gather | solution.py:36
  96.8 166.4 %reduce-scatter.12.cloned.1.call-start = ((), (), s32[]{:S(2)}) async-start(), calls=%async_computation.10 | async-start | bytes 1966080 | tf_op jit(solution)/shard_map/reduce_scatter | solution.py:40
  133.4 133.9 %copy-start.5 = (f32[1024,768]{0,1:T(8,128)}, f32[1024,768]{0,1:T(8,128)S(1)}, u32[]{:S(2)}) copy-start(f32[1024,768]{0,1:T(8,128)S(1)} %get-tuple-element.109) | copy-start | bytes 9437188
  219.5 6.8 %copy-start.58 = (bf16[768,768]{1,0:T(8,128)(2,1)S(1)}, bf16[768,768]{1,0:T(8,128)(2,1)}, u32[]{:S(2)}) copy-start(bf16[768,768]{1,0:T(8,128)(2,1)} %all-gather.18.cloned.1.call-done) | copy-start | bytes 3538948
  228.9 79.2 %reduce-scatter.18.cloned.1.call-start = ((), (), s32[]{:S(2)}) async-start(), calls=%async_computation.17 | async-start | bytes 2654208 | tf_op jit(solution)/shard_map/reduce_scatter | solution.py:192
  240.2 107.8 %all-gather.22.cloned.1.call-start = ((), (), s32[]{:S(2)}) async-start(), calls=%async_computation.11 | async-start | bytes 1966080 | tf_op jit(solution)/shard_map/all_gather | solution.py:36
  270.0 80.0 %copy-start.4 = (f32[3,512,512]{1,2,0:T(8,128)S(1)}, f32[3,512,512]{1,2,0:T(8,128)}, u32[]{:S(2)}) copy-start(f32[3,512,512]{1,2,0:T(8,128)} %copy-done.3) | copy-start | bytes 9437188
  270.1 108.2 %all-gather.28.cloned.1.call-start = ((), (), s32[]{:S(2)}) async-start(), calls=%async_computation.15 | async-start | bytes 1474560 | tf_op jit(solution)/shard_map/all_gather | solution.py:194
  308.1 109.7 %reduce-scatter.16.cloned.1.call-start = ((), (), s32[]{:S(2)}) async-start(), calls=%async_computation.16 | async-start | bytes 1327104 | tf_op jit(solution)/shard_map/reduce_scatter | solution.py:193
  353.1 10.9 %copy-start.25 = (bf16[3,64,512]{2,1,0:T(8,128)(2,1)}, bf16[3,64,512]{2,1,0:T(8,128)(2,1)S(1)}, u32[]{:S(2)}) copy-start(bf16[3,64,512]{2,1,0:T(8,128)(2,1)S(1)} %fusion.52) | copy-start | bytes 589828
  367.2 92.8 %reduce-scatter.14.cloned.1.call-start = ((), (), s32[]{:S(2)}) async-start(), calls=%async_computation.12 | async-start | bytes 1966080 | tf_op jit(solution)/shard_map/reduce_scatter | solution.py:40
  371.1 133.9 %reduce-scatter.10.cloned.1.call-start = ((), (), s32[]{:S(2)}) async-start(), calls=%async_computation.9 | async-start | bytes 1966080 | tf_op jit(solution)/shard_map/reduce_scatter | solution.py:40
  441.8 18.2 %copy-start.38 = (f32[256]{0:T(256)S(1)}, f32[256]{0:T(256)}, u32[]{:S(2)}) copy-start(f32[256]{0:T(256)} %broadcast_multiply_fusion.2) | copy-start | bytes 3076
  441.8 21.2 %copy-start.43 = (f32[1,768]{1,0:T(1,128)S(1)}, f32[1,768]{1,0:T(1,128)}, u32[]{:S(2)}) copy-start(f32[1,768]{1,0:T(1,128)} %reshape.279) | copy-start | bytes 9220
  441.8 21.2 %copy-start.44 = (f32[1,768]{1,0:T(1,128)S(1)}, f32[1,768]{1,0:T(1,128)}, u32[]{:S(2)}) copy-start(f32[1,768]{1,0:T(1,128)} %reshape.278) | copy-start | bytes 9220
  441.9 63.2 %copy-start.9 = (bf16[256,768]{0,1:T(8,128)(2,1)S(1)}, bf16[256,768]{0,1:T(8,128)(2,1)}, u32[]{:S(2)}) copy-start(bf16[256,768]{0,1:T(8,128)(2,1)} %reduce-scatter.12.cloned.1.call-done) | copy-start | bytes 1179652
  441.9 63.1 %copy-start.10 = (bf16[1,256,768]{1,2,0:T(8,128)(2,1)S(1)}, bf16[1,256,768]{1,2,0:T(8,128)(2,1)}, u32[]{:S(2)}) copy-start(bf16[1,256,768]{1,2,0:T(8,128)(2,1)} %copy.134) | copy-start | bytes 1179652
  441.9 63.1 %copy-start.32 = (f32[256]{0:T(256)S(1)}, f32[256]{0:T(256)}, u32[]{:S(2)}) copy-start(f32[256]{0:T(256)} %broadcast_multiply_fusion.3) | copy-start | bytes 3076
  441.9 63.1 %copy-start.40 = (f32[256]{0:T(256)S(1)}, f32[256]{0:T(256)}, u32[]{:S(2)}) copy-start(f32[256]{0:T(256)} %copy-done.39) | copy-start | bytes 3076
  441.9 63.1 %copy-start.42 = (f32[256]{0:T(256)S(1)}, f32[256]{0:T(256)}, u32[]{:S(2)}) copy-start(f32[256]{0:T(256)} %copy-done.41) | copy-start | bytes 3076
  441.9 63.1 %copy-start.46 = (f32[256]{0:T(256)S(1)}, f32[256]{0:T(256)}, u32[]{:S(2)}) copy-start(f32[256]{0:T(256)} %copy-done.45) | copy-start | bytes 3076
  460.0 48.9 %copy-start.1 = (bf16[384,768]{1,0:T(8,128)(2,1)S(1)}, bf16[384,768]{1,0:T(8,128)(2,1)}, u32[]{:S(2)}) copy-start(bf16[384,768]{1,0:T(8,128)(2,1)} %param.14) | copy-start | bytes 1769476
  (44 other events, 123.4 us)
Sparse Core Ops, SparseCore 0:
  10.2 40.3 all-gather.23
  53.1 26.4 all-gather.13
  92.2 37.0 all-gather.15
  131.6 22.9 all-gather.17
  156.9 24.0 all-gather.19
  182.4 37.0 all-gather.25
  229.0 34.1 reduce-scatter.11
  266.6 41.4 reduce-scatter.17
  310.3 37.6 all-gather.21
  349.5 28.7 all-gather.27
  381.8 35.8 reduce-scatter.15
  419.9 40.0 reduce-scatter.13
  462.3 35.2 reduce-scatter.9
